TPU v7x, 32 devices: a whole 2x2x4 slice. The times are simulated.
32 devices in a mesh: seq: 16 (over z, x, core), head: 2 (over y).
Axes of the slice: x: 2, y: 2, z: 4, core: 2. Of those that a mesh axis runs over, the one named last changes fastest.
Arguments:
- queries: bfloat16 [4096, 512], P('seq', 'head'), may hold values from -6 to 6
- key_rows: bfloat16 [4096, 512], P('seq', 'head'), may hold values from -6 to 6
- value_rows: bfloat16 [4096, 1024], P('seq', 'head'), may hold values from -6 to 6
- log_decay: float32 [2, 4096], P('head', 'seq'), may hold values from -1.5 to 0, as said below
- upstream: bfloat16 [4096, 1024], P(('seq', 'head')), may hold values from -6 to 6
- norm_gain: float32 [2, 512], P('head'), may hold values from 0.25 to 1.75
Outputs:
- query_grad: bfloat16 [4096, 512], P('seq', 'head')
- key_grad: bfloat16 [4096, 512], P('seq', 'head')
- value_grad: bfloat16 [4096, 1024], P('seq', 'head')
- gain_grad: float32 [2, 512], P('head')
- bias_grad: float32 [2, 512], P('head')
Inputs may be any that keep to these rules, and one draw needn't show every extreme that they name: log_decay is never positive.
All inputs are finite; a program needn't handle non-finite values.
Results may differ from a plain program's by a relative error of at most 0.0067.
Values may be sent and summed in bfloat16 or wider, within the bound.
A program may use at most 64 MiB of HBM per device.

v0:
```python
import jax
import jax.numpy as jnp
from jax import lax
from jax.sharding import PartitionSpec as P

norm_eps = 1e-05


def from_behind(block, axis, distance):
    devices = range(lax.axis_size(axis))
    route = [(i - distance, i) for i in devices if i - distance in devices]
    return lax.ppermute(block, axis, route)


def decay_matrix(running):
    length = running.shape[0]
    positions = jnp.arange(length)
    lower = positions[:, None] >= positions[None, :]
    spread = jnp.where(lower, running[:, None] - running[None, :], 0.0)
    return jnp.where(lower, jnp.exp(spread), 0.0)


def block_terms(query_rows, key_rows, value_rows, decays):
    scaling = query_rows.shape[1] ** (-0.5)
    running = jnp.cumsum(decays)
    block_total = running[-1]
    decay_mat = decay_matrix(running)
    weights = (
        jnp.dot(query_rows, key_rows.T, preferred_element_type=jnp.float32) * scaling * decay_mat
    ).astype(jnp.bfloat16)
    head_decay = jnp.exp(running)
    query_decayed = (query_rows.astype(jnp.float32) * head_decay[:, None]).astype(jnp.bfloat16)
    tail_decay = jnp.exp(block_total - running)
    key_decayed = (key_rows.astype(jnp.float32) * tail_decay[:, None]).astype(jnp.bfloat16)
    local_state = jnp.dot(key_decayed.T, value_rows, preferred_element_type=jnp.float32)
    return (
        decay_mat,
        weights,
        head_decay,
        query_decayed,
        tail_decay,
        local_state,
        jnp.exp(block_total),
    )


def norm_backward(terms, value_rows, state_in, upstream_rows, gain_row):
    decay_mat, weights, head_decay, query_decayed, tail_decay, local_state, block_decay = terms
    scaling = query_decayed.shape[1] ** (-0.5)
    state_low = state_in.astype(jnp.bfloat16)
    output = jnp.dot(weights, value_rows, preferred_element_type=jnp.float32) + scaling * jnp.dot(
        query_decayed, state_low, preferred_element_type=jnp.float32
    )
    centered = output - jnp.mean(output, axis=-1, keepdims=True)
    inverse = lax.rsqrt(jnp.mean(centered * centered, axis=-1, keepdims=True) + norm_eps)
    normed = centered * inverse
    cotangent = upstream_rows.astype(jnp.float32)
    gain_part = jnp.sum(cotangent * normed, axis=0)
    bias_part = jnp.sum(cotangent, axis=0)
    scaled = cotangent * gain_row
    grad_output = (
        inverse
        * (
            scaled
            - jnp.mean(scaled, axis=-1, keepdims=True)
            - normed * jnp.mean(scaled * normed, axis=-1, keepdims=True)
        )
    ).astype(jnp.bfloat16)
    back_local = scaling * jnp.dot(query_decayed.T, grad_output, preferred_element_type=jnp.float32)
    return (grad_output, back_local, gain_part, bias_part)


def retention_backward(terms, query_rows, key_rows, value_rows, grad_output, state_in, state_after):
    decay_mat, weights, head_decay, query_decayed, tail_decay, local_state, block_decay = terms
    scaling = query_rows.shape[1] ** (-0.5)
    state_low = state_in.astype(jnp.bfloat16)
    after_low = state_after.astype(jnp.bfloat16)
    grad_weights = (
        jnp.dot(grad_output, value_rows.T, preferred_element_type=jnp.float32) * scaling * decay_mat
    ).astype(jnp.bfloat16)
    query_grad = jnp.dot(grad_weights, key_rows, preferred_element_type=jnp.float32) + (
        scaling * head_decay
    )[:, None] * jnp.dot(grad_output, state_low.T, preferred_element_type=jnp.float32)
    key_grad = jnp.dot(grad_weights.T, query_rows, preferred_element_type=jnp.float32) + tail_decay[
        :, None
    ] * jnp.dot(value_rows, after_low.T, preferred_element_type=jnp.float32)
    value_grad = jnp.dot(weights.T, grad_output, preferred_element_type=jnp.float32) + tail_decay[
        :, None
    ] * jnp.dot(key_rows, after_low, preferred_element_type=jnp.float32)
    return (
        query_grad.astype(jnp.bfloat16),
        key_grad.astype(jnp.bfloat16),
        value_grad.astype(jnp.bfloat16),
    )


def combine_carry(earlier, later_part):
    return (earlier[0] * later_part[0], later_part[0][:, None, None] * earlier[1] + later_part[1])


def to_heads(array, head_count):
    length, width_all = array.shape
    return array.reshape(length, head_count, width_all // head_count).transpose(1, 0, 2)


def from_heads(array):
    head_count, length, head_width = array.shape
    return array.transpose(1, 0, 2).reshape(length, head_count * head_width)


def forward_levels(pair_now):
    for level_num in range(lax.axis_size("seq").bit_length() - 1):
        earlier = from_behind((pair_now[0], pair_now[1]), "seq", 1 << level_num)
        pair_now = combine_carry(earlier, pair_now)
    return (
        from_behind(pair_now[0].astype(jnp.bfloat16), "seq", 1).astype(jnp.float32),
        from_behind(pair_now[1].astype(jnp.bfloat16), "seq", 1).astype(jnp.float32),
    )


def backward_levels(pair_now):
    for level_num in range(lax.axis_size("seq").bit_length() - 1):
        earlier = from_behind((pair_now[0], pair_now[1]), "seq", -(1 << level_num))
        pair_now = combine_carry(earlier, pair_now)
    return (
        from_behind(pair_now[0].astype(jnp.bfloat16), "seq", -1).astype(jnp.float32),
        from_behind(pair_now[1].astype(jnp.bfloat16), "seq", -1).astype(jnp.float32),
    )


def shards(queries, key_rows, value_rows, log_decay, upstream, norm_gain):
    head_count = norm_gain.shape[0]
    query_heads = to_heads(queries, head_count)
    key_heads = to_heads(key_rows, head_count)
    value_heads = to_heads(value_rows, head_count)
    terms = jax.vmap(block_terms)(query_heads, key_heads, value_heads, log_decay)
    states_in = forward_levels((terms[6], terms[5]))[1]
    cotangent = lax.all_to_all(upstream, "head", split_axis=1, concat_axis=0, tiled=True)
    cotangent_heads = to_heads(cotangent, head_count)
    grad_output, back_local, gain_part, bias_part = jax.vmap(norm_backward)(
        terms, value_heads, states_in, cotangent_heads, norm_gain
    )
    gain_total, bias_total = lax.psum((gain_part, bias_part), "seq")
    states_after = backward_levels((terms[6], back_local))[1]
    gradients = jax.vmap(retention_backward)(
        terms, query_heads, key_heads, value_heads, grad_output, states_in, states_after
    )
    norm_factor = (queries.shape[0] * lax.axis_size("seq")) ** (-0.5)
    return (
        from_heads(gradients[0]),
        from_heads(gradients[1]),
        from_heads(gradients[2]),
        gain_total * norm_factor,
        bias_total * norm_factor,
    )


def solution(mesh):
    in_specs = (
        P("seq", "head"),
        P("seq", "head"),
        P("seq", "head"),
        P("head", "seq"),
        P(("seq", "head"), None),
        P("head", None),
    )
    out_specs = (
        P("seq", "head"),
        P("seq", "head"),
        P("seq", "head"),
        P("head", None),
        P("head", None),
    )
    return jax.shard_map(shards, mesh=mesh, in_specs=in_specs, out_specs=out_specs, check_vma=False)
```

profile of v0, /device:TPU:15, one launch (start us, length us, event | category | flops | bytes accessed | tf_op | source)
XLA Modules:
  0.0 181.6 jit_solution(2918795372849868973)
XLA Ops:
  0.6 0.0 copy-start
  0.7 0.7 copy-done.5
  1.4 0.3 reduce-window.6
  1.7 0.2 slice_reduce_fusion
  1.9 0.2 reduce-window.9
  2.0 0.1 broadcast_multiply_fusion.2
  2.1 0.1 broadcast.125
  2.2 0.6 slice.13
  2.8 0.6 slice.12
  4.7 1.2 convolution_bitcast_fusion
  5.9 3.7 %collective-permute-start.3 = (f32[1,256,512]{2,1,0:T(8,128)S(1)}, f32[1,256,512]{2,1,0:T(8,128)S(1)}, u32[]{:S(2)}, u32[]{:S(2)}) collective-permute-start(f32[1,256,512]{2,1,0:T(8,128)S(1)} %convolution_bitcast_fusion), channel_id=1, source_target_pairs={{0,2},{2,4},{4,6},{6,8},{8,10},{10,12},{12,14},{14,16},{16,18},{18... | collective-permute-start | bytes 1572872 | tf_op jit(solution)/shard_map/ppermute | solution.py:12
  9.7 6.1 %collective-permute-done.3 = f32[1,256,512]{2,1,0:T(8,128)S(1)} collective-permute-done((f32[1,256,512]{2,1,0:T(8,128)S(1)}, f32[1,256,512]{2,1,0:T(8,128)S(1)}, u32[]{:S(2)}, u32[]{:S(2)}) %collective-permute-start.3) | collective-permute-done | bytes 524320 | tf_op jit(solution)/shard_map/ppermute | solution.py:12
  15.8 0.1 multiply_add_fusion.5
  15.9 3.1 %collective-permute-start.4 = (f32[1,256,512]{2,1,0:T(8,128)S(1)}, f32[1,256,512]{2,1,0:T(8,128)S(1)}, u32[]{:S(2)}, u32[]{:S(2)}) collective-permute-start(f32[1,256,512]{2,1,0:T(8,128)S(1)} %multiply_add_fusion.5), channel_id=1, source_target_pairs={{0,4},{2,6},{4,8},{6,10},{8,12},{10,14},{12,16},{14,18},{16,20},{1... | collective-permute-start | bytes 1572872 | tf_op jit(solution)/shard_map/ppermute | solution.py:12
  19.0 9.0 %collective-permute-start = (f32[1]{0:T(128)}, f32[1]{0:T(128)}, u32[]{:S(2)}, u32[]{:S(2)}) collective-permute-start(f32[1]{0:T(128)} %bitcast.9), channel_id=1, source_target_pairs={{0,2},{2,4},{4,6},{6,8},{8,10},{10,12},{12,14},{14,16},{16,18},{18... | collective-permute-start | bytes 20 | tf_op jit(solution)/shard_map/ppermute | solution.py:12
  28.6 1.3 collective-permute-done.4
  29.9 0.1 multiply_add_fusion.4
  29.9 3.2 %collective-permute-start.5 = (f32[1,256,512]{2,1,0:T(8,128)S(1)}, f32[1,256,512]{2,1,0:T(8,128)S(1)}, u32[]{:S(2)}, u32[]{:S(2)}) collective-permute-start(f32[1,256,512]{2,1,0:T(8,128)S(1)} %multiply_add_fusion.4), channel_id=1, source_target_pairs={{0,8},{2,10},{4,12},{6,14},{8,16},{10,18},{12,20},{14,22},{16,24},... | collective-permute-start | bytes 1572872 | tf_op jit(solution)/shard_map/ppermute | solution.py:12
  33.2 9.0 %collective-permute-start.1 = (f32[1]{0:T(128)}, f32[1]{0:T(128)}, u32[]{:S(2)}, u32[]{:S(2)}) collective-permute-start(f32[1]{0:T(128)} %mul.248), channel_id=1, source_target_pairs={{0,4},{2,6},{4,8},{6,10},{8,12},{10,14},{12,16},{14,18},{16,20},{1... | collective-permute-start | bytes 20 | tf_op jit(solution)/shard_map/ppermute | solution.py:12
  42.8 0.2 collective-permute-done.5
  43.0 0.1 multiply_add_fusion.3
  43.1 2.9 %collective-permute-start.6 = (f32[1,256,512]{2,1,0:T(8,128)S(1)}, f32[1,256,512]{2,1,0:T(8,128)S(1)}, u32[]{:S(2)}, u32[]{:S(2)}) collective-permute-start(f32[1,256,512]{2,1,0:T(8,128)S(1)} %multiply_add_fusion.3), channel_id=1, source_target_pairs={{0,16},{2,18},{4,20},{6,22},{8,24},{10,26},{12,28},{14,30},{1,17},... | collective-permute-start | bytes 1572872 | tf_op jit(solution)/shard_map/ppermute | solution.py:12
  46.1 0.7 copy.21
  46.8 3.8 %all-to-all-start = ((bf16[128,2,512]{2,0,1:T(8,128)(2,1)}), bf16[128,2,512]{2,0,1:T(8,128)(2,1)S(1)}, u32[]{:S(2)}, u32[]{:S(2)}) async-start(bf16[128,2,512]{2,0,1:T(8,128)(2,1)} %bitcast.107), calls=%async_computation | async-start | bytes 524288 | tf_op jit(solution)/shard_map/all_to_all | solution.py:138
  50.6 0.2 fusion.10
  50.8 0.2 fusion.31
  51.0 16.6 %collective-permute-start.2 = (f32[1]{0:T(128)}, f32[1]{0:T(128)}, u32[]{:S(2)}, u32[]{:S(2)}) collective-permute-start(f32[1]{0:T(128)} %mul.249), channel_id=1, source_target_pairs={{0,8},{2,10},{4,12},{6,14},{8,16},{10,18},{12,20},{14,22},{16,24},... | collective-permute-start | bytes 20 | tf_op jit(solution)/shard_map/ppermute | solution.py:12
  68.3 0.0 copy-start.4
  68.3 0.1 add_convert_fusion.1
  68.4 7.0 %collective-permute-start.7 = (bf16[1,256,512]{2,1,0:T(8,128)(2,1)S(1)}, bf16[1,256,512]{2,1,0:T(8,128)(2,1)S(1)}, u32[]{:S(2)}, u32[]{:S(2)}) collective-permute-start(bf16[1,256,512]{2,1,0:T(8,128)(2,1)S(1)} %add_convert_fusion.1), channel_id=1, source_target_pairs={{0,2},{2,4},{4,6},{6,8},{8,10},{10,12},{12,14},{14,16},{16,18},{18... | collective-permute-start | bytes 786440 | tf_op jit(solution)/shard_map/ppermute | solution.py:12
  75.5 0.1 convert_reduce_fusion
  75.6 3.1 %collective-permute-done.7 = bf16[1,256,512]{2,1,0:T(8,128)(2,1)S(1)} collective-permute-done((bf16[1,256,512]{2,1,0:T(8,128)(2,1)S(1)}, bf16[1,256,512]{2,1,0:T(8,128)(2,1)S(1)}, u32[]{:S(2)}, u32[]{:S(2)}) %collective-permute-start.7) | collective-permute-done | bytes 262176 | tf_op jit(solution)/shard_map/ppermute | solution.py:12
  78.7 0.4 fusion.30
  79.1 0.2 multiply_reduce_fusion
  79.3 0.3 fusion.21
  79.6 0.2 fusion.18
  79.8 0.3 fusion.2
  80.2 1.9 %collective-permute-start.11 = (f32[1,256,512]{2,1,0:T(8,128)S(1)}, f32[1,256,512]{2,1,0:T(8,128)S(1)}, u32[]{:S(2)}, u32[]{:S(2)}) collective-permute-start(f32[1,256,512]{2,1,0:T(8,128)S(1)} %fusion.2), channel_id=1, source_target_pairs={{2,0},{4,2},{6,4},{8,6},{10,8},{12,10},{14,12},{16,14},{18,16},{20... | collective-permute-start | bytes 1572872 | tf_op jit(solution)/shard_map/ppermute | solution.py:12
  82.1 10.2 %collective-permute-done.11 = f32[1,256,512]{2,1,0:T(8,128)S(1)} collective-permute-done((f32[1,256,512]{2,1,0:T(8,128)S(1)}, f32[1,256,512]{2,1,0:T(8,128)S(1)}, u32[]{:S(2)}, u32[]{:S(2)}) %collective-permute-start.11) | collective-permute-done | bytes 524320 | tf_op jit(solution)/shard_map/ppermute | solution.py:12
  92.3 0.1 multiply_add_fusion.2
  92.4 1.9 %collective-permute-start.12 = (f32[1,256,512]{2,1,0:T(8,128)S(1)}, f32[1,256,512]{2,1,0:T(8,128)S(1)}, u32[]{:S(2)}, u32[]{:S(2)}) collective-permute-start(f32[1,256,512]{2,1,0:T(8,128)S(1)} %multiply_add_fusion.2), channel_id=1, source_target_pairs={{4,0},{6,2},{8,4},{10,6},{12,8},{14,10},{16,12},{18,14},{20,16},{2... | collective-permute-start | bytes 1572872 | tf_op jit(solution)/shard_map/ppermute | solution.py:12
  94.4 2.9 %collective-permute-start.8 = (f32[1]{0:T(128)}, f32[1]{0:T(128)}, u32[]{:S(2)}, u32[]{:S(2)}) collective-permute-start(f32[1]{0:T(128)} %bitcast.9), channel_id=1, source_target_pairs={{2,0},{4,2},{6,4},{8,6},{10,8},{12,10},{14,12},{16,14},{18,16},{20... | collective-permute-start | bytes 20 | tf_op jit(solution)/shard_map/ppermute | solution.py:12
  97.2 7.4 %collective-permute-done.8 = f32[1]{0:T(128)} collective-permute-done((f32[1]{0:T(128)}, f32[1]{0:T(128)}, u32[]{:S(2)}, u32[]{:S(2)}) %collective-permute-start.8) | collective-permute-done | bytes 36 | tf_op jit(solution)/shard_map/ppermute | solution.py:12
  105.3 1.4 collective-permute-done.12
  106.7 0.1 multiply_add_fusion.1
  106.8 1.9 %collective-permute-start.13 = (f32[1,256,512]{2,1,0:T(8,128)S(1)}, f32[1,256,512]{2,1,0:T(8,128)S(1)}, u32[]{:S(2)}, u32[]{:S(2)}) collective-permute-start(f32[1,256,512]{2,1,0:T(8,128)S(1)} %multiply_add_fusion.1), channel_id=1, source_target_pairs={{8,0},{10,2},{12,4},{14,6},{16,8},{18,10},{20,12},{22,14},{24,16},... | collective-permute-start | bytes 1572872 | tf_op jit(solution)/shard_map/ppermute | solution.py:12
  108.7 2.6 %collective-permute-start.9 = (f32[1]{0:T(128)}, f32[1]{0:T(128)}, u32[]{:S(2)}, u32[]{:S(2)}) collective-permute-start(f32[1]{0:T(128)} %mul.285), channel_id=1, source_target_pairs={{4,0},{6,2},{8,4},{10,6},{12,8},{14,10},{16,12},{18,14},{20,16},{2... | collective-permute-start | bytes 20 | tf_op jit(solution)/shard_map/ppermute | solution.py:12
  111.3 11.8 %collective-permute-done.9 = f32[1]{0:T(128)} collective-permute-done((f32[1]{0:T(128)}, f32[1]{0:T(128)}, u32[]{:S(2)}, u32[]{:S(2)}) %collective-permute-start.9) | collective-permute-done | bytes 36 | tf_op jit(solution)/shard_map/ppermute | solution.py:12
  123.8 2.6 %collective-permute-start.10 = (f32[1]{0:T(128)}, f32[1]{0:T(128)}, u32[]{:S(2)}, u32[]{:S(2)}) collective-permute-start(f32[1]{0:T(128)} %mul.286), channel_id=1, source_target_pairs={{8,0},{10,2},{12,4},{14,6},{16,8},{18,10},{20,12},{22,14},{24,16},... | collective-permute-start | bytes 20 | tf_op jit(solution)/shard_map/ppermute | solution.py:12
  126.4 1.6 collective-permute-done.10
  128.7 0.3 fusion.11
  128.9 0.1 multiply_add_fusion
  129.0 1.3 collective-permute-start.14
  130.3 0.2 fusion.33
  130.6 39.5 %all-reduce = (f32[1,512]{1,0:T(1,128)S(1)}, f32[1,512]{1,0:T(1,128)S(1)}) all-reduce(f32[1,512]{1,0:T(1,128)S(1)} %bitcast.113, f32[1,512]{1,0:T(1,128)S(1)} %bitcast.112), channel_id=1, replica_groups=mesh['seq'=16,'head'=2] {'seq'}, use_global_device_ids=true, to_apply=%region_7.8 | all-reduce | flops 1024 | bytes 8192 | tf_op jit(solution)/shard_map/psum | solution.py:143
  170.0 0.2 fusion.32
  170.2 0.2 fusion.34
  170.5 0.1 add_convert_fusion
  170.6 1.9 %collective-permute-start.15 = (bf16[1,256,512]{2,1,0:T(8,128)(2,1)S(1)}, bf16[1,256,512]{2,1,0:T(8,128)(2,1)S(1)}, u32[]{:S(2)}, u32[]{:S(2)}) collective-permute-start(bf16[1,256,512]{2,1,0:T(8,128)(2,1)S(1)} %add_convert_fusion), channel_id=1, source_target_pairs={{2,0},{4,2},{6,4},{8,6},{10,8},{12,10},{14,12},{16,14},{18,16},{20... | collective-permute-start | bytes 786440 | tf_op jit(solution)/shard_map/ppermute | solution.py:12
  172.5 0.6 broadcast_multiply_fusion
  173.1 0.9 fusion.12
  174.0 5.7 %collective-permute-done.15 = bf16[1,256,512]{2,1,0:T(8,128)(2,1)S(1)} collective-permute-done((bf16[1,256,512]{2,1,0:T(8,128)(2,1)S(1)}, bf16[1,256,512]{2,1,0:T(8,128)(2,1)S(1)}, u32[]{:S(2)}, u32[]{:S(2)}) %collective-permute-start.15) | collective-permute-done | bytes 262176 | tf_op jit(solution)/shard_map/ppermute | solution.py:12
  179.7 0.9 fusion.4
  180.7 0.9 fusion.13
  (22 shorter events, 0.1 us)
Async XLA Ops:
  0.6 4.0 %copy-start = (bf16[256,512]{1,0:T(8,128)(2,1)S(1)}, bf16[256,512]{1,0:T(8,128)(2,1)}, u32[]{:S(2)}) copy-start(bf16[256,512]{1,0:T(8,128)(2,1)} %param.8) | copy-start | bytes 786436
  0.6 0.7 copy-start.5
  5.9 9.8 %collective-permute-start.3 = (f32[1,256,512]{2,1,0:T(8,128)S(1)}, f32[1,256,512]{2,1,0:T(8,128)S(1)}, u32[]{:S(2)}, u32[]{:S(2)}) collective-permute-start(f32[1,256,512]{2,1,0:T(8,128)S(1)} %convolution_bitcast_fusion), channel_id=1, source_target_pairs={{0,2},{2,4},{4,6},{6,8},{8,10},{10,12},{12,14},{14,16},{16,18},{18... | collective-permute-start | bytes 1572872 | tf_op jit(solution)/shard_map/ppermute | solution.py:12
  15.9 14.0 %collective-permute-start.4 = (f32[1,256,512]{2,1,0:T(8,128)S(1)}, f32[1,256,512]{2,1,0:T(8,128)S(1)}, u32[]{:S(2)}, u32[]{:S(2)}) collective-permute-start(f32[1,256,512]{2,1,0:T(8,128)S(1)} %multiply_add_fusion.5), channel_id=1, source_target_pairs={{0,4},{2,6},{4,8},{6,10},{8,12},{10,14},{12,16},{14,18},{16,20},{1... | collective-permute-start | bytes 1572872 | tf_op jit(solution)/shard_map/ppermute | solution.py:12
  19.0 9.0 %collective-permute-start = (f32[1]{0:T(128)}, f32[1]{0:T(128)}, u32[]{:S(2)}, u32[]{:S(2)}) collective-permute-start(f32[1]{0:T(128)} %bitcast.9), channel_id=1, source_target_pairs={{0,2},{2,4},{4,6},{6,8},{8,10},{10,12},{12,14},{14,16},{16,18},{18... | collective-permute-start | bytes 20 | tf_op jit(solution)/shard_map/ppermute | solution.py:12
  29.9 13.1 %collective-permute-start.5 = (f32[1,256,512]{2,1,0:T(8,128)S(1)}, f32[1,256,512]{2,1,0:T(8,128)S(1)}, u32[]{:S(2)}, u32[]{:S(2)}) collective-permute-start(f32[1,256,512]{2,1,0:T(8,128)S(1)} %multiply_add_fusion.4), channel_id=1, source_target_pairs={{0,8},{2,10},{4,12},{6,14},{8,16},{10,18},{12,20},{14,22},{16,24},... | collective-permute-start | bytes 1572872 | tf_op jit(solution)/shard_map/ppermute | solution.py:12
  33.2 9.0 %collective-permute-start.1 = (f32[1]{0:T(128)}, f32[1]{0:T(128)}, u32[]{:S(2)}, u32[]{:S(2)}) collective-permute-start(f32[1]{0:T(128)} %mul.248), channel_id=1, source_target_pairs={{0,4},{2,6},{4,8},{6,10},{8,12},{10,14},{12,16},{14,18},{16,20},{1... | collective-permute-start | bytes 20 | tf_op jit(solution)/shard_map/ppermute | solution.py:12
  43.0 3.0 %copy-start.3 = (bf16[128,1024]{1,0:T(8,128)(2,1)S(1)}, bf16[128,1024]{1,0:T(8,128)(2,1)}, u32[]{:S(2)}) copy-start(bf16[128,1024]{1,0:T(8,128)(2,1)} %param.10) | copy-start | bytes 786436
  43.1 25.2 %collective-permute-start.6 = (f32[1,256,512]{2,1,0:T(8,128)S(1)}, f32[1,256,512]{2,1,0:T(8,128)S(1)}, u32[]{:S(2)}, u32[]{:S(2)}) collective-permute-start(f32[1,256,512]{2,1,0:T(8,128)S(1)} %multiply_add_fusion.3), channel_id=1, source_target_pairs={{0,16},{2,18},{4,20},{6,22},{8,24},{10,26},{12,28},{14,30},{1,17},... | collective-permute-start | bytes 1572872 | tf_op jit(solution)/shard_map/ppermute | solution.py:12
  46.8 3.8 %copy-start.1 = (bf16[256,256]{1,0:T(8,128)(2,1)S(1)}, bf16[256,256]{1,0:T(8,128)(2,1)}, u32[]{:S(2)}) copy-start(bf16[256,256]{1,0:T(8,128)(2,1)} %param.6) | copy-start | bytes 393220
  46.8 3.8 %copy-start.2 = (bf16[256,256]{1,0:T(8,128)(2,1)S(1)}, bf16[256,256]{1,0:T(8,128)(2,1)}, u32[]{:S(2)}) copy-start(bf16[256,256]{1,0:T(8,128)(2,1)} %param.7) | copy-start | bytes 393220
  46.8 28.7 %all-to-all-start = ((bf16[128,2,512]{2,0,1:T(8,128)(2,1)}), bf16[128,2,512]{2,0,1:T(8,128)(2,1)S(1)}, u32[]{:S(2)}, u32[]{:S(2)}) async-start(bf16[128,2,512]{2,0,1:T(8,128)(2,1)} %bitcast.107), calls=%async_computation | async-start | bytes 524288 | tf_op jit(solution)/shard_map/all_to_all | solution.py:138
  51.0 16.6 %collective-permute-start.2 = (f32[1]{0:T(128)}, f32[1]{0:T(128)}, u32[]{:S(2)}, u32[]{:S(2)}) collective-permute-start(f32[1]{0:T(128)} %mul.249), channel_id=1, source_target_pairs={{0,8},{2,10},{4,12},{6,14},{8,16},{10,18},{12,20},{14,22},{16,24},... | collective-permute-start | bytes 20 | tf_op jit(solution)/shard_map/ppermute | solution.py:12
  68.3 7.1 %copy-start.4 = (f32[1,512]{1,0:T(1,128)S(1)}, f32[1,512]{1,0:T(1,128)}, u32[]{:S(2)}) copy-start(f32[1,512]{1,0:T(1,128)} %param.11) | copy-start | bytes 6148
  68.4 10.3 %collective-permute-start.7 = (bf16[1,256,512]{2,1,0:T(8,128)(2,1)S(1)}, bf16[1,256,512]{2,1,0:T(8,128)(2,1)S(1)}, u32[]{:S(2)}, u32[]{:S(2)}) collective-permute-start(bf16[1,256,512]{2,1,0:T(8,128)(2,1)S(1)} %add_convert_fusion.1), channel_id=1, source_target_pairs={{0,2},{2,4},{4,6},{6,8},{8,10},{10,12},{12,14},{14,16},{16,18},{18... | collective-permute-start | bytes 786440 | tf_op jit(solution)/shard_map/ppermute | solution.py:12
  80.2 12.1 %collective-permute-start.11 = (f32[1,256,512]{2,1,0:T(8,128)S(1)}, f32[1,256,512]{2,1,0:T(8,128)S(1)}, u32[]{:S(2)}, u32[]{:S(2)}) collective-permute-start(f32[1,256,512]{2,1,0:T(8,128)S(1)} %fusion.2), channel_id=1, source_target_pairs={{2,0},{4,2},{6,4},{8,6},{10,8},{12,10},{14,12},{16,14},{18,16},{20... | collective-permute-start | bytes 1572872 | tf_op jit(solution)/shard_map/ppermute | solution.py:12
  92.4 14.2 %collective-permute-start.12 = (f32[1,256,512]{2,1,0:T(8,128)S(1)}, f32[1,256,512]{2,1,0:T(8,128)S(1)}, u32[]{:S(2)}, u32[]{:S(2)}) collective-permute-start(f32[1,256,512]{2,1,0:T(8,128)S(1)} %multiply_add_fusion.2), channel_id=1, source_target_pairs={{4,0},{6,2},{8,4},{10,6},{12,8},{14,10},{16,12},{18,14},{20,16},{2... | collective-permute-start | bytes 1572872 | tf_op jit(solution)/shard_map/ppermute | solution.py:12
  94.4 10.3 %collective-permute-start.8 = (f32[1]{0:T(128)}, f32[1]{0:T(128)}, u32[]{:S(2)}, u32[]{:S(2)}) collective-permute-start(f32[1]{0:T(128)} %bitcast.9), channel_id=1, source_target_pairs={{2,0},{4,2},{6,4},{8,6},{10,8},{12,10},{14,12},{16,14},{18,16},{20... | collective-permute-start | bytes 20 | tf_op jit(solution)/shard_map/ppermute | solution.py:12
  106.8 22.2 %collective-permute-start.13 = (f32[1,256,512]{2,1,0:T(8,128)S(1)}, f32[1,256,512]{2,1,0:T(8,128)S(1)}, u32[]{:S(2)}, u32[]{:S(2)}) collective-permute-start(f32[1,256,512]{2,1,0:T(8,128)S(1)} %multiply_add_fusion.1), channel_id=1, source_target_pairs={{8,0},{10,2},{12,4},{14,6},{16,8},{18,10},{20,12},{22,14},{24,16},... | collective-permute-start | bytes 1572872 | tf_op jit(solution)/shard_map/ppermute | solution.py:12
  108.7 14.4 %collective-permute-start.9 = (f32[1]{0:T(128)}, f32[1]{0:T(128)}, u32[]{:S(2)}, u32[]{:S(2)}) collective-permute-start(f32[1]{0:T(128)} %mul.285), channel_id=1, source_target_pairs={{4,0},{6,2},{8,4},{10,6},{12,8},{14,10},{16,12},{18,14},{20,16},{2... | collective-permute-start | bytes 20 | tf_op jit(solution)/shard_map/ppermute | solution.py:12
  123.8 4.2 %collective-permute-start.10 = (f32[1]{0:T(128)}, f32[1]{0:T(128)}, u32[]{:S(2)}, u32[]{:S(2)}) collective-permute-start(f32[1]{0:T(128)} %mul.286), channel_id=1, source_target_pairs={{8,0},{10,2},{12,4},{14,6},{16,8},{18,10},{20,12},{22,14},{24,16},... | collective-permute-start | bytes 20 | tf_op jit(solution)/shard_map/ppermute | solution.py:12
  129.0 41.4 %collective-permute-start.14 = (f32[1,256,512]{2,1,0:T(8,128)S(1)}, f32[1,256,512]{2,1,0:T(8,128)S(1)}, u32[]{:S(2)}, u32[]{:S(2)}) collective-permute-start(f32[1,256,512]{2,1,0:T(8,128)S(1)} %multiply_add_fusion), channel_id=1, source_target_pairs={{16,0},{18,2},{20,4},{22,6},{24,8},{26,10},{28,12},{30,14},{17,1},... | collective-permute-start | bytes 1572872 | tf_op jit(solution)/shard_map/ppermute | solution.py:12
  170.6 9.1 %collective-permute-start.15 = (bf16[1,256,512]{2,1,0:T(8,128)(2,1)S(1)}, bf16[1,256,512]{2,1,0:T(8,128)(2,1)S(1)}, u32[]{:S(2)}, u32[]{:S(2)}) collective-permute-start(bf16[1,256,512]{2,1,0:T(8,128)(2,1)S(1)} %add_convert_fusion), channel_id=1, source_target_pairs={{2,0},{4,2},{6,4},{8,6},{10,8},{12,10},{14,12},{16,14},{18,16},{20... | collective-permute-start | bytes 786440 | tf_op jit(solution)/shard_map/ppermute | solution.py:12
where the time goes:
time: 182 us
  starting transfers between devices  75.4 us (41%)
  waiting for transfers between devices  48.8 us (27%)
  blocking collectives  39.5 us (22%)
  between operations  6.12 us (3%)
  matrix products  6.06 us (3%)
  local copies, waits for them, and re-layouts  2.89 us (2%)
  other arithmetic  2.83 us (2%)
    ppermute x16, starting transfers between devices, from_behind(): return lax.ppermute(block, axis, route)  71.7 us
    ppermute x16, waiting for transfers between devices, from_behind(): return lax.ppermute(block, axis, route)  48.8 us
    psum x1, blocking collectives, shards(): gain_total, bias_total = lax.psum((gain_part, bias_part), 'seq')  39.5 us
    all_to_all x1, starting transfers between devices, shards(): lax.all_to_all(upstream, 'head', split_axis=1, concat_axis=0, tiled=True)  3.77 us
  transfers between devices with their start and end apart: 17, of which 10 were waited for; matrix products, arithmetic and copies ran while one was open for 2% of the time, Pallas kernels for 0%

commit v1 on v0

v1 whole, which is shorter than its diff:
```python
import functools

import jax
import jax.numpy as jnp
from jax import lax
from jax.experimental import pallas as pl
from jax.experimental.pallas import tpu as pltpu
from jax.sharding import PartitionSpec as P

norm_eps = 1e-05
f32, bf16 = jnp.float32, jnp.bfloat16
PIECES = 2


def dot_nn(a, b):
    return lax.dot_general(a, b, (((1,), (0,)), ((), ())), preferred_element_type=f32)


def dot_nt(a, b):
    return lax.dot_general(a, b, (((1,), (1,)), ((), ())), preferred_element_type=f32)


def dot_tn(a, b):
    return lax.dot_general(a, b, (((0,), (0,)), ((), ())), preferred_element_type=f32)


def kernel(
    seq_total, head_total, members, pieces,
    q_hbm, k_hbm, v_hbm, decay_hbm, up_hbm, gain_hbm,
    qg_hbm, kg_hbm, vg_hbm, gg_hbm, bg_hbm,
    q_ref, k_ref, v_ref, decay_ref, gain_ref, up_ref, total_ref,
    lsend, lrecv, carry, csend, psend, state, stat_in, stat_z, stat_sum,
    qg_ref, kg_ref, vg_ref, gg_ref, bg_ref,
    load_sem, total_sem, up_sem, scatter_sem, chain_sem, spread_sem, stat_sem, statz_sem, out_sem,
):
    me = lax.axis_index("seq")
    head = lax.axis_index("head")
    groups = seq_total // members
    z = me // members
    r = me % members
    rows, dk = q_ref.shape
    dv = v_ref.shape[1]
    scaling = dk ** (-0.5)

    def member(d):
        return lax.rem(r + d, members)

    def remote(src, dst, sems, at, device):
        return pltpu.make_async_remote_copy(
            src_ref=src, dst_ref=dst, send_sem=sems.at[(0, *at)], recv_sem=sems.at[(1, *at)],
            device_id=device, device_id_type=pl.DeviceIdType.MESH,
        )

    def in_group(d):
        return {"seq": z * members + member(d)}

    def other_group(d):
        return {"seq": lax.rem(z + d, groups) * members + r}

    def other_head(d):
        return {"head": lax.rem(head + d, head_total)}

    up_own = up_hbm.at[:, pl.ds(pl.multiple_of(head * dv, dv), dv)]
    loads = [
        pltpu.make_async_copy(src, dst, load_sem.at[i])
        for i, (src, dst) in enumerate((
            (decay_hbm, decay_ref), (k_hbm, k_ref), (v_hbm, v_ref), (q_hbm, q_ref),
            (gain_hbm, gain_ref), (up_own, up_ref.at[head]),
        ))
    ]
    for load in loads:
        load.start()

    barrier = pltpu.get_barrier_semaphore()
    partners = (
        [in_group(d) for d in range(1, members)]
        + [other_group(d) for d in range(1, groups)]
        + [other_head(d) for d in range(1, head_total)]
    )
    for partner in partners:
        pl.semaphore_signal(barrier, inc=1, device_id=partner, device_id_type=pl.DeviceIdType.MESH)

    loads[0].wait()
    decays = decay_ref[...]
    at_row = lax.broadcasted_iota(jnp.int32, (rows, rows), 0)
    at_col = lax.broadcasted_iota(jnp.int32, (rows, rows), 1)
    lower = at_row >= at_col
    running = jnp.sum(jnp.where(lower, decays, 0.0), axis=1, keepdims=True)
    running_row = jnp.sum(jnp.where(at_row == at_col, running, 0.0), axis=0, keepdims=True)
    block_total = running[rows - 1 : rows, :]
    tail_decay = jnp.exp(block_total - running)
    head_decay = jnp.exp(running)
    total_ref[r] = jnp.broadcast_to(block_total, total_ref.shape[1:])
    loads[1].wait()
    loads[2].wait()
    keys, values = k_ref[...], v_ref[...]
    key_decayed = (keys.astype(f32) * tail_decay).astype(bf16)
    local_state = dot_tn(key_decayed, values)

    def scatter_copy(way, d, s):
        return remote(
            lsend.at[way, member(d), s], lrecv.at[way, r, s], scatter_sem, (way, d, s), in_group(d)
        )

    def scatter_arrival(way, d, s):
        return remote(
            lsend.at[way, member(d), s], lrecv.at[way, member(members - d), s], scatter_sem,
            (way, d, s), in_group(d),
        )

    def chain_copy(way, s):
        step = 1 if way == 0 else groups - 1
        return remote(csend.at[way, s], carry.at[way, s], chain_sem, (way, s), other_group(step))

    def spread_copy(way, d, s):
        return remote(
            psend.at[way, member(d), s], state.at[way, r, s], spread_sem, (way, d, s), in_group(d)
        )

    def spread_arrival(way, d, s):
        return remote(
            psend.at[way, member(d), s], state.at[way, member(members - d), s], spread_sem,
            (way, d, s), in_group(d),
        )

    def total_copy(d):
        return remote(total_ref.at[r], total_ref.at[r], total_sem, (d,), in_group(d))

    def total_arrival(d):
        slot = total_ref.at[member(members - d)]
        return remote(slot, slot, total_sem, (d,), in_group(d))

    def up_copy(d):
        whom = lax.rem(head + d, head_total)
        return remote(
            up_hbm.at[:, pl.ds(pl.multiple_of(whom * dv, dv), dv)], up_ref.at[head], up_sem, (d,),
            other_head(d),
        )

    def up_arrival(d):
        whom = lax.rem(head + head_total - d, head_total)
        return remote(up_hbm.at[:, pl.ds(0, dv)], up_ref.at[whom], up_sem, (d,), other_head(d))

    def stat_copy(d):
        return remote(stat_in.at[r], stat_in.at[r], stat_sem, (d,), in_group(d))

    def stat_arrival(d):
        slot = stat_in.at[member(members - d)]
        return remote(slot, slot, stat_sem, (d,), in_group(d))

    def statz_copy(d):
        return remote(stat_z.at[z], stat_z.at[z], statz_sem, (d,), other_group(d))

    def statz_arrival(d):
        slot = stat_z.at[lax.rem(z + groups - d, groups)]
        return remote(slot, slot, statz_sem, (d,), other_group(d))

    def scatter(way, local):
        lsend[way] = local.astype(bf16).reshape(lsend.shape[1:])
        for s in range(pieces):
            for d in range(1, members):
                scatter_copy(way, d, s).start()
        lrecv[way, r] = lsend[way, r]

    def chain(way, group_decays):
        order = range(members) if way == 0 else range(members - 1, -1, -1)
        first, last = (0, groups - 1) if way == 0 else (groups - 1, 0)
        whole = functools.reduce(lambda a, b: a * b, group_decays)

        @pl.when(z == first)
        def _():
            carry[way] = jnp.zeros(carry.shape[1:], bf16)

        for s in range(pieces):
            for d in range(1, members):
                scatter_arrival(way, d, s).wait_recv()
            total = None
            for m in order:
                part = lrecv[way, m, s].astype(f32)
                total = part if total is None else group_decays[m] * total + part

            @pl.when(z != first)
            def _():
                chain_copy(way, s).wait_recv()

            csend[way, s] = (whole * carry[way, s].astype(f32) + total).astype(bf16)

            @pl.when(z != last)
            def _():
                chain_copy(way, s).start()

            now = carry[way, s].astype(f32)
            for at, m in enumerate(order):
                psend[way, m, s] = now.astype(bf16)
                if at < members - 1:
                    now = group_decays[m] * now + lrecv[way, m, s].astype(f32)
            for d in range(1, members):
                spread_copy(way, d, s).start()
            state[way, r, s] = psend[way, r, s]

    def gathered(way):
        for s in range(pieces):
            for d in range(1, members):
                spread_arrival(way, d, s).wait_recv()
        return state[way].reshape(dk, dv)

    pl.semaphore_wait(barrier, len(partners))
    for d in range(1, members):
        total_copy(d).start()
    scatter(0, local_state)
    for d in range(1, head_total):
        up_copy(d).start()

    loads[3].wait()
    queries = q_ref[...]
    decay_mat = jnp.where(lower, jnp.exp(jnp.where(lower, running - running_row, 0.0)), 0.0)
    decay_mat = decay_mat * scaling
    weights = (dot_nt(queries, keys) * decay_mat).astype(bf16)
    query_decayed = (queries.astype(f32) * head_decay).astype(bf16)
    inner = dot_nn(weights, values)

    for d in range(1, members):
        total_arrival(d).wait_recv()
    group_decays = [jnp.exp(total_ref[m, 0:1, 0:1]) for m in range(members)]
    chain(0, group_decays)

    loads[4].wait()
    loads[5].wait()
    for d in range(1, head_total):
        up_arrival(d).wait_recv()
    cotangent = up_ref[...].reshape(rows, dv).astype(f32)
    scaled = cotangent * gain_ref[...]
    scaled_mean = jnp.mean(scaled, axis=-1, keepdims=True)

    state_in = gathered(0)
    output = inner + scaling * dot_nn(query_decayed, state_in)
    centered = output - jnp.mean(output, axis=-1, keepdims=True)
    inverse = lax.rsqrt(jnp.mean(centered * centered, axis=-1, keepdims=True) + norm_eps)
    normed = centered * inverse
    grad_output = (
        inverse * (scaled - scaled_mean - normed * jnp.mean(scaled * normed, axis=-1, keepdims=True))
    ).astype(bf16)
    scatter(1, scaling * dot_tn(query_decayed, grad_output))

    stat_in[r, 0:1, :] = jnp.sum(cotangent * normed, axis=0, keepdims=True)
    stat_in[r, 1:2, :] = jnp.sum(cotangent, axis=0, keepdims=True)
    for d in range(1, members):
        stat_copy(d).start()
    grad_weights = (dot_nt(grad_output, values) * decay_mat).astype(bf16)
    qg_ref[...] = (
        dot_nn(grad_weights, keys) + (scaling * head_decay) * dot_nt(grad_output, state_in)
    ).astype(bf16)
    outs = [
        pltpu.make_async_copy(src, dst, out_sem.at[i])
        for i, (src, dst) in enumerate((
            (qg_ref, qg_hbm), (kg_ref, kg_hbm), (vg_ref, vg_hbm), (gg_ref, gg_hbm), (bg_ref, bg_hbm),
        ))
    ]
    outs[0].start()

    chain(1, group_decays)

    key_inner = dot_tn(grad_weights, queries)
    value_inner = dot_tn(weights, grad_output)
    for d in range(1, members):
        stat_arrival(d).wait_recv()
    both = stat_in[0]
    for m in range(1, members):
        both = both + stat_in[m]
    stat_z[z] = both
    for d in range(1, groups):
        statz_copy(d).start()

    state_after = gathered(1)
    kg_ref[...] = (key_inner + tail_decay * dot_nt(values, state_after)).astype(bf16)
    outs[1].start()
    vg_ref[...] = (value_inner + tail_decay * dot_nn(keys, state_after)).astype(bf16)
    outs[2].start()

    for d in range(1, groups):
        statz_arrival(d).wait_recv()
    both = stat_z[0]
    for m in range(1, groups):
        both = both + stat_z[m]
    both = both * ((rows * seq_total) ** (-0.5))
    gg_ref[...] = both[0:1, :]
    bg_ref[...] = both[1:2, :]
    outs[3].start()
    outs[4].start()

    for d in range(1, members):
        total_copy(d).wait_send()
        stat_copy(d).wait_send()
        for way in range(2):
            for s in range(pieces):
                scatter_copy(way, d, s).wait_send()
                spread_copy(way, d, s).wait_send()
    for d in range(1, head_total):
        up_copy(d).wait_send()
    for d in range(1, groups):
        statz_copy(d).wait_send()
    for way, last in ((0, groups - 1), (1, 0)):

        @pl.when(z != last)
        def _():
            for s in range(pieces):
                chain_copy(way, s).wait_send()

    for out in outs:
        out.wait()


def shards(queries, key_rows, value_rows, log_decay, upstream, norm_gain):
    seq_total, head_total = lax.axis_size("seq"), lax.axis_size("head")
    members = 4 if seq_total % 4 == 0 else 1
    groups = seq_total // members
    rows, dk = queries.shape
    dv = value_rows.shape[1]
    pieces = PIECES
    piece = (pieces, dk // members // pieces, dv)
    any_space = pl.BlockSpec(memory_space=pl.ANY)
    dma = pltpu.SemaphoreType.DMA
    return pl.pallas_call(
        functools.partial(kernel, seq_total, head_total, members, pieces),
        out_shape=(
            jax.ShapeDtypeStruct((rows, dk), bf16),
            jax.ShapeDtypeStruct((rows, dk), bf16),
            jax.ShapeDtypeStruct((rows, dv), bf16),
            jax.ShapeDtypeStruct((1, dv), f32),
            jax.ShapeDtypeStruct((1, dv), f32),
        ),
        in_specs=[any_space] * 6,
        out_specs=(any_space,) * 5,
        scratch_shapes=[
            pltpu.VMEM((rows, dk), bf16),
            pltpu.VMEM((rows, dk), bf16),
            pltpu.VMEM((rows, dv), bf16),
            pltpu.VMEM((1, rows), f32),
            pltpu.VMEM((1, dv), f32),
            pltpu.VMEM((head_total, rows // head_total, dv), bf16),
            pltpu.VMEM((members, 8, 128), f32),
            pltpu.VMEM((2, members, *piece), bf16),
            pltpu.VMEM((2, members, *piece), bf16),
            pltpu.VMEM((2, *piece), bf16),
            pltpu.VMEM((2, *piece), bf16),
            pltpu.VMEM((2, members, *piece), bf16),
            pltpu.VMEM((2, members, *piece), bf16),
            pltpu.VMEM((members, 2, dv), f32),
            pltpu.VMEM((groups, 2, dv), f32),
            pltpu.VMEM((8, dv), f32),
            pltpu.VMEM((rows, dk), bf16),
            pltpu.VMEM((rows, dk), bf16),
            pltpu.VMEM((rows, dv), bf16),
            pltpu.VMEM((1, dv), f32),
            pltpu.VMEM((1, dv), f32),
            dma((6,)),
            dma((2, members)),
            dma((2, max(head_total, 2))),
            dma((2, 2, members, pieces)),
            dma((2, 2, pieces)),
            dma((2, 2, members, pieces)),
            dma((2, members)),
            dma((2, max(groups, 2))),
            dma((5,)),
        ],
        compiler_params=pltpu.CompilerParams(
            collective_id=0, has_side_effects=True, vmem_limit_bytes=40 * 2**20
        ),
    )(queries, key_rows, value_rows, log_decay, upstream, norm_gain)


def solution(mesh):
    in_specs = (
        P("seq", "head"),
        P("seq", "head"),
        P("seq", "head"),
        P("head", "seq"),
        P(("seq", "head"), None),
        P("head", None),
    )
    out_specs = (
        P("seq", "head"),
        P("seq", "head"),
        P("seq", "head"),
        P("head", None),
        P("head", None),
    )
    return jax.shard_map(shards, mesh=mesh, in_specs=in_specs, out_specs=out_specs, check_vma=False)
```

time: 182 us -> 49.9 us (0.27)
  the two profiles are of different devices: /device:TPU:15 before, /device:TPU:0 now
where the time goes in v1:
time: 49.9 us; the launch traced here: 49.6 us
  Pallas kernels  40.7 us (82%)
  local copies, waits for them, and re-layouts  8.23 us (16%)
  between operations  0.66 us (1%)
    pallas_call x1, Pallas kernels, shards(): pl.pallas_call(functools.partial(kernel, seq_total, head_total, members,...  40.7 us
    unnamed x17, local copies, waits for them, and re-layouts  8.23 us

profile of v1, /device:TPU:0, one launch (start us, length us, event | category | flops | bytes accessed | tf_op | source)
XLA Modules:
  0.0 49.6 jit_solution(16734979019619497022)
XLA Ops:
  0.6 0.0 copy-start
  0.6 0.9 %copy-done = bf16[256,512]{1,0:T(8,128)(2,1)S(1)} copy-done((bf16[256,512]{1,0:T(8,128)(2,1)S(1)}, bf16[256,512]{1,0:T(8,128)(2,1)}, u32[]{:S(2)}) %copy-start) | copy-done | bytes 262168
  1.6 0.0 copy-start.1
  1.6 0.9 %copy-done.1 = bf16[128,1024]{1,0:T(8,128)(2,1)S(1)} copy-done((bf16[128,1024]{1,0:T(8,128)(2,1)S(1)}, bf16[128,1024]{1,0:T(8,128)(2,1)}, u32[]{:S(2)}) %copy-start.1) | copy-done | bytes 262168
  2.5 0.0 copy-start.2
  2.5 0.9 %copy-done.2 = bf16[256,256]{1,0:T(8,128)(2,1)S(1)} copy-done((bf16[256,256]{1,0:T(8,128)(2,1)S(1)}, bf16[256,256]{1,0:T(8,128)(2,1)}, u32[]{:S(2)}) %copy-start.2) | copy-done | bytes 131096
  3.4 0.0 copy-start.3
  3.4 0.9 %copy-done.3 = bf16[256,256]{1,0:T(8,128)(2,1)S(1)} copy-done((bf16[256,256]{1,0:T(8,128)(2,1)S(1)}, bf16[256,256]{1,0:T(8,128)(2,1)}, u32[]{:S(2)}) %copy-start.3) | copy-done | bytes 131096
  4.3 0.0 copy-start.4
  4.3 0.7 %copy-done.4 = f32[1,512]{1,0:T(1,128)S(1)} copy-done((f32[1,512]{1,0:T(1,128)S(1)}, f32[1,512]{1,0:T(1,128)}, u32[]{:S(2)}) %copy-start.4) | copy-done | bytes 2072
  5.0 0.0 copy-start.5
  5.0 0.7 %copy-done.5 = f32[1,256]{1,0:T(1,128)S(1)} copy-done((f32[1,256]{1,0:T(1,128)S(1)}, f32[1,256]{1,0:T(1,128)}, u32[]{:S(2)}) %copy-start.5) | copy-done | bytes 1048
  5.7 40.7 %shard_map.101 = (bf16[256,256]{1,0:T(8,128)(2,1)S(1)}, bf16[256,256]{1,0:T(8,128)(2,1)S(1)}, bf16[256,512]{1,0:T(8,128)(2,1)S(1)}, f32[1,512]{1,0:T(1,128)S(1)}, f32[1,512]{1,0:T(1,128)S(1)}) custom-call(bf16[256,256]{1,0:T(8,128)(2,1)S(1)} %copy-done.2, bf16[256,256]{1,0:T(8,128)(2,1)S(1)} %copy-done.3, bf16[256,512]{1,0:T(8,128)(2,1)S(1)} %copy-done, ...), custom_call_target="tpu_custom_call" | custom-call | tf_op jit(solution)/shard_map/pallas_call | solution.py:323
  46.4 0.7 %copy.16 = bf16[256,256]{1,0:T(8,128)(2,1)} copy(bf16[256,256]{1,0:T(8,128)(2,1)S(1)} %get-tuple-element.10) | data formatting | bytes 262144
  47.1 0.7 %copy.17 = bf16[256,256]{1,0:T(8,128)(2,1)} copy(bf16[256,256]{1,0:T(8,128)(2,1)S(1)} %get-tuple-element.11) | data formatting | bytes 262144
  47.8 0.7 %copy.18 = bf16[256,512]{1,0:T(8,128)(2,1)} copy(bf16[256,512]{1,0:T(8,128)(2,1)S(1)} %get-tuple-element.12) | data formatting | bytes 524288
  48.5 0.6 %copy.19 = f32[1,512]{1,0:T(1,128)} copy(f32[1,512]{1,0:T(1,128)S(1)} %get-tuple-element.13) | data formatting | bytes 4096
  49.0 0.6 %copy.20 = f32[1,512]{1,0:T(1,128)} copy(f32[1,512]{1,0:T(1,128)S(1)} %get-tuple-element.14) | data formatting | bytes 4096
Async XLA Ops:
  0.6 1.0 %copy-start = (bf16[256,512]{1,0:T(8,128)(2,1)S(1)}, bf16[256,512]{1,0:T(8,128)(2,1)}, u32[]{:S(2)}) copy-start(bf16[256,512]{1,0:T(8,128)(2,1)} %v_hbm.1) | copy-start | bytes 786436
  1.6 0.9 %copy-start.1 = (bf16[128,1024]{1,0:T(8,128)(2,1)S(1)}, bf16[128,1024]{1,0:T(8,128)(2,1)}, u32[]{:S(2)}) copy-start(bf16[128,1024]{1,0:T(8,128)(2,1)} %up_hbm.1) | copy-start | bytes 786436
  2.5 0.9 %copy-start.2 = (bf16[256,256]{1,0:T(8,128)(2,1)S(1)}, bf16[256,256]{1,0:T(8,128)(2,1)}, u32[]{:S(2)}) copy-start(bf16[256,256]{1,0:T(8,128)(2,1)} %q_hbm.1) | copy-start | bytes 393220
  3.4 0.9 %copy-start.3 = (bf16[256,256]{1,0:T(8,128)(2,1)S(1)}, bf16[256,256]{1,0:T(8,128)(2,1)}, u32[]{:S(2)}) copy-start(bf16[256,256]{1,0:T(8,128)(2,1)} %k_hbm.1) | copy-start | bytes 393220
  4.3 0.7 %copy-start.4 = (f32[1,512]{1,0:T(1,128)S(1)}, f32[1,512]{1,0:T(1,128)}, u32[]{:S(2)}) copy-start(f32[1,512]{1,0:T(1,128)} %gain_hbm.1) | copy-start | bytes 6148
  5.0 0.7 %copy-start.5 = (f32[1,256]{1,0:T(1,128)S(1)}, f32[1,256]{1,0:T(1,128)}, u32[]{:S(2)}) copy-start(f32[1,256]{1,0:T(1,128)} %decay_hbm.1) | copy-start | bytes 3076

commit v2 on v1

--- a/solution.py
+++ b/solution.py
@@ -9,7 +9,7 @@
 
 norm_eps = 1e-05
 f32, bf16 = jnp.float32, jnp.bfloat16
-PIECES = 2
+PIECES = 4
 
 
 def dot_nn(a, b):
@@ -27,11 +27,10 @@
 def kernel(
     seq_total, head_total, members, pieces,
     q_hbm, k_hbm, v_hbm, decay_hbm, up_hbm, gain_hbm,
-    qg_hbm, kg_hbm, vg_hbm, gg_hbm, bg_hbm,
+    qg_ref, kg_ref, vg_ref, gg_ref, bg_ref,
     q_ref, k_ref, v_ref, decay_ref, gain_ref, up_ref, total_ref,
-    lsend, lrecv, carry, csend, psend, state, stat_in, stat_z, stat_sum,
-    qg_ref, kg_ref, vg_ref, gg_ref, bg_ref,
-    load_sem, total_sem, up_sem, scatter_sem, chain_sem, spread_sem, stat_sem, statz_sem, out_sem,
+    turned, lsend, lrecv, carry, csend, psend, state, stat_in, stat_z, stat_sum,
+    load_sem, total_sem, up_sem, scatter_sem, chain_sem, spread_sem, stat_sem, statz_sem,
 ):
     me = lax.axis_index("seq")
     head = lax.axis_index("head")
@@ -95,7 +94,7 @@
     loads[2].wait()
     keys, values = k_ref[...], v_ref[...]
     key_decayed = (keys.astype(f32) * tail_decay).astype(bf16)
-    local_state = dot_tn(key_decayed, values)
+    turned[0] = key_decayed.T.reshape(turned.shape[1:])
 
     def scatter_copy(way, d, s):
         return remote(
@@ -155,12 +154,15 @@
         slot = stat_z.at[lax.rem(z + groups - d, groups)]
         return remote(slot, slot, statz_sem, (d,), other_group(d))
 
-    def scatter(way, local):
-        lsend[way] = local.astype(bf16).reshape(lsend.shape[1:])
-        for s in range(pieces):
-            for d in range(1, members):
-                scatter_copy(way, d, s).start()
-        lrecv[way, r] = lsend[way, r]
+    def scatter(way, right):
+        for d in [members // 2, *(d for d in range(1, members) if d != members // 2), 0]:
+            part = dot_nn(turned[way, member(d)], right).astype(bf16).reshape(lsend.shape[2:])
+            if d:
+                lsend[way, member(d)] = part
+                for s in range(pieces):
+                    scatter_copy(way, d, s).start()
+            else:
+                lrecv[way, r] = part
 
     def chain(way, group_decays):
         order = range(members) if way == 0 else range(members - 1, -1, -1)
@@ -207,7 +209,7 @@
     pl.semaphore_wait(barrier, len(partners))
     for d in range(1, members):
         total_copy(d).start()
-    scatter(0, local_state)
+    scatter(0, values)
     for d in range(1, head_total):
         up_copy(d).start()
 
@@ -218,6 +220,7 @@
     weights = (dot_nt(queries, keys) * decay_mat).astype(bf16)
     query_decayed = (queries.astype(f32) * head_decay).astype(bf16)
     inner = dot_nn(weights, values)
+    turned[1] = (scaling * query_decayed.astype(f32)).astype(bf16).T.reshape(turned.shape[1:])
 
     for d in range(1, members):
         total_arrival(d).wait_recv()
@@ -235,12 +238,11 @@
     state_in = gathered(0)
     output = inner + scaling * dot_nn(query_decayed, state_in)
     centered = output - jnp.mean(output, axis=-1, keepdims=True)
+    along = jnp.mean(scaled * centered, axis=-1, keepdims=True)
     inverse = lax.rsqrt(jnp.mean(centered * centered, axis=-1, keepdims=True) + norm_eps)
     normed = centered * inverse
-    grad_output = (
-        inverse * (scaled - scaled_mean - normed * jnp.mean(scaled * normed, axis=-1, keepdims=True))
-    ).astype(bf16)
-    scatter(1, scaling * dot_tn(query_decayed, grad_output))
+    grad_output = (inverse * (scaled - scaled_mean - normed * (along * inverse))).astype(bf16)
+    scatter(1, grad_output)
 
     stat_in[r, 0:1, :] = jnp.sum(cotangent * normed, axis=0, keepdims=True)
     stat_in[r, 1:2, :] = jnp.sum(cotangent, axis=0, keepdims=True)
@@ -250,14 +252,6 @@
     qg_ref[...] = (
         dot_nn(grad_weights, keys) + (scaling * head_decay) * dot_nt(grad_output, state_in)
     ).astype(bf16)
-    outs = [
-        pltpu.make_async_copy(src, dst, out_sem.at[i])
-        for i, (src, dst) in enumerate((
-            (qg_ref, qg_hbm), (kg_ref, kg_hbm), (vg_ref, vg_hbm), (gg_ref, gg_hbm), (bg_ref, bg_hbm),
-        ))
-    ]
-    outs[0].start()
-
     chain(1, group_decays)
 
     key_inner = dot_tn(grad_weights, queries)
@@ -273,9 +267,7 @@
 
     state_after = gathered(1)
     kg_ref[...] = (key_inner + tail_decay * dot_nt(values, state_after)).astype(bf16)
-    outs[1].start()
     vg_ref[...] = (value_inner + tail_decay * dot_nn(keys, state_after)).astype(bf16)
-    outs[2].start()
 
     for d in range(1, groups):
         statz_arrival(d).wait_recv()
@@ -285,8 +277,6 @@
     both = both * ((rows * seq_total) ** (-0.5))
     gg_ref[...] = both[0:1, :]
     bg_ref[...] = both[1:2, :]
-    outs[3].start()
-    outs[4].start()
 
     for d in range(1, members):
         total_copy(d).wait_send()
@@ -306,8 +296,18 @@
             for s in range(pieces):
                 chain_copy(way, s).wait_send()
 
-    for out in outs:
-        out.wait()
+
+def write_out(*refs):
+    *pairs, sems = refs
+    half = len(pairs) // 2
+    copies = [
+        pltpu.make_async_copy(src, dst, sems.at[i])
+        for i, (src, dst) in enumerate(zip(pairs[:half], pairs[half:]))
+    ]
+    for copy in copies:
+        copy.start()
+    for copy in copies:
+        copy.wait()
 
 
 def shards(queries, key_rows, value_rows, log_decay, upstream, norm_gain):
@@ -318,19 +318,21 @@
     dv = value_rows.shape[1]
     pieces = PIECES
     piece = (pieces, dk // members // pieces, dv)
-    any_space = pl.BlockSpec(memory_space=pl.ANY)
+    in_hbm = pl.BlockSpec(memory_space=pltpu.HBM)
+    in_vmem = pl.BlockSpec(memory_space=pltpu.VMEM)
+    shapes = (
+        jax.ShapeDtypeStruct((rows, dk), bf16),
+        jax.ShapeDtypeStruct((rows, dk), bf16),
+        jax.ShapeDtypeStruct((rows, dv), bf16),
+        jax.ShapeDtypeStruct((1, dv), f32),
+        jax.ShapeDtypeStruct((1, dv), f32),
+    )
     dma = pltpu.SemaphoreType.DMA
-    return pl.pallas_call(
+    results = pl.pallas_call(
         functools.partial(kernel, seq_total, head_total, members, pieces),
-        out_shape=(
-            jax.ShapeDtypeStruct((rows, dk), bf16),
-            jax.ShapeDtypeStruct((rows, dk), bf16),
-            jax.ShapeDtypeStruct((rows, dv), bf16),
-            jax.ShapeDtypeStruct((1, dv), f32),
-            jax.ShapeDtypeStruct((1, dv), f32),
-        ),
-        in_specs=[any_space] * 6,
-        out_specs=(any_space,) * 5,
+        out_shape=shapes,
+        in_specs=[in_hbm] * 6,
+        out_specs=(in_vmem,) * 5,
         scratch_shapes=[
             pltpu.VMEM((rows, dk), bf16),
             pltpu.VMEM((rows, dk), bf16),
@@ -339,6 +341,7 @@
             pltpu.VMEM((1, dv), f32),
             pltpu.VMEM((head_total, rows // head_total, dv), bf16),
             pltpu.VMEM((members, 8, 128), f32),
+            pltpu.VMEM((2, members, dk // members, rows), bf16),
             pltpu.VMEM((2, members, *piece), bf16),
             pltpu.VMEM((2, members, *piece), bf16),
             pltpu.VMEM((2, *piece), bf16),
@@ -348,11 +351,6 @@
             pltpu.VMEM((members, 2, dv), f32),
             pltpu.VMEM((groups, 2, dv), f32),
             pltpu.VMEM((8, dv), f32),
-            pltpu.VMEM((rows, dk), bf16),
-            pltpu.VMEM((rows, dk), bf16),
-            pltpu.VMEM((rows, dv), bf16),
-            pltpu.VMEM((1, dv), f32),
-            pltpu.VMEM((1, dv), f32),
             dma((6,)),
             dma((2, members)),
             dma((2, max(head_total, 2))),
@@ -361,12 +359,19 @@
             dma((2, 2, members, pieces)),
             dma((2, members)),
             dma((2, max(groups, 2))),
-            dma((5,)),
         ],
         compiler_params=pltpu.CompilerParams(
-            collective_id=0, has_side_effects=True, vmem_limit_bytes=40 * 2**20
+            collective_id=0, has_side_effects=True, vmem_limit_bytes=62 * 2**20
         ),
     )(queries, key_rows, value_rows, log_decay, upstream, norm_gain)
+    return pl.pallas_call(
+        write_out,
+        out_shape=shapes,
+        in_specs=[in_vmem] * 5,
+        out_specs=(in_hbm,) * 5,
+        scratch_shapes=[dma((5,))],
+        compiler_params=pltpu.CompilerParams(vmem_limit_bytes=62 * 2**20),
+    )(*results)
 
 
 def solution(mesh):

time: 49.9 us -> 42.6 us (0.85)
  local copies, waits for them, and re-layouts: 8.23 us -> 0 us
  Pallas kernels: 40.7 us -> 41.8 us
    unnamed x17 -> x0, local copies, waits for them, and re-layouts: 8.23 us -> none
    pallas_call x0 -> x1, Pallas kernels: none -> 1.93 us  [shards(): pl.pallas_call(write_out, out_shape=shapes, in_specs=[in_vmem] * 5, out_s...]
    pallas_call x1, Pallas kernels: 40.7 us -> 39.9 us  [shards(): pl.pallas_call(functools.partial(kernel, seq_total, head_total, members,...]
where the time goes in v2:
time: 42.6 us; the launch traced here: 42.5 us
  Pallas kernels  41.8 us (98%)
  between operations  0.64 us (2%)
    pallas_call x1, Pallas kernels, shards(): pl.pallas_call(functools.partial(kernel, seq_total, head_total, members,...  39.9 us
    pallas_call x1, Pallas kernels, shards(): pl.pallas_call(write_out, out_shape=shapes, in_specs=[in_vmem] * 5, out_s...  1.93 us

profile of v2, /device:TPU:0, one launch (start us, length us, event | category | flops | bytes accessed | tf_op | source)
XLA Modules:
  0.0 42.5 jit_solution(1706367583377828817)
XLA Ops:
  0.6 39.9 %shard_map.101 = (bf16[256,256]{1,0:T(8,128)(2,1)}, bf16[256,256]{1,0:T(8,128)(2,1)}, bf16[256,512]{1,0:T(8,128)(2,1)}, f32[1,512]{1,0:T(1,128)}, f32[1,512]{1,0:T(1,128)}) custom-call(bf16[256,256]{1,0:T(8,128)(2,1)} %q_hbm.1, bf16[256,256]{1,0:T(8,128)(2,1)} %k_hbm.1, bf16[256,512]{1,0:T(8,128)(2,1)} %v_hbm.1, f32[1,256]{1,0:T(1,128)} %decay_hbm.1, ...), custom_call_target="tpu_custom_call" | custom-call | tf_op jit(solution)/shard_map/pallas_call | solution.py:331
  40.5 1.9 %shard_map.102 = (bf16[256,256]{1,0:T(8,128)(2,1)}, bf16[256,256]{1,0:T(8,128)(2,1)}, bf16[256,512]{1,0:T(8,128)(2,1)}, f32[1,512]{1,0:T(1,128)}, f32[1,512]{1,0:T(1,128)}) custom-call(bf16[256,256]{1,0:T(8,128)(2,1)} %get-tuple-element.10.refs_0_, bf16[256,256]{1,0:T(8,128)(2,1)} %get-tuple-element.11.refs_1_, bf16[256,512]{1,0:T(8,128)(2,1)} %get-tuple-element.12.refs_2_, ...), custom_call_target="tpu_custom_call" | custom-call | tf_op jit(solution)/shard_map/pallas_call | solution.py:367

commit v3 on v2

--- a/solution.py
+++ b/solution.py
@@ -28,9 +28,9 @@
     seq_total, head_total, members, pieces,
     q_hbm, k_hbm, v_hbm, decay_hbm, up_hbm, gain_hbm,
     qg_ref, kg_ref, vg_ref, gg_ref, bg_ref,
-    q_ref, k_ref, v_ref, decay_ref, gain_ref, up_ref, total_ref,
+    q_ref, k_ref, v_ref, decay_ref, gain_ref, up_ref, total_ref, span_ref,
     turned, lsend, lrecv, carry, csend, psend, state, stat_in, stat_z, stat_sum,
-    load_sem, total_sem, up_sem, scatter_sem, chain_sem, spread_sem, stat_sem, statz_sem,
+    load_sem, total_sem, up_sem, scatter_sem, chain_sem, spread_sem, stat_sem, statz_sem, span_sem,
 ):
     me = lax.axis_index("seq")
     head = lax.axis_index("head")
@@ -107,9 +107,28 @@
             (way, d, s), in_group(d),
         )
 
-    def chain_copy(way, s):
-        step = 1 if way == 0 else groups - 1
-        return remote(csend.at[way, s], carry.at[way, s], chain_sem, (way, s), other_group(step))
+    def sends_to(way, d):
+        return z + d < groups if way == 0 else z - d >= 0
+
+    def chain_copy(way, d, s):
+        return remote(
+            csend.at[way, s], carry.at[way, z, s], chain_sem, (way, d, s),
+            other_group(d if way == 0 else groups - d),
+        )
+
+    def chain_arrival(way, d, s):
+        source = lax.rem(z + (groups - d if way == 0 else d), groups)
+        return remote(
+            csend.at[way, s], carry.at[way, source, s], chain_sem, (way, d, s),
+            other_group(d if way == 0 else groups - d),
+        )
+
+    def span_copy(d):
+        return remote(span_ref.at[z], span_ref.at[z], span_sem, (d,), other_group(d))
+
+    def span_arrival(d):
+        slot = span_ref.at[lax.rem(z + groups - d, groups)]
+        return remote(slot, slot, span_sem, (d,), other_group(d))
 
     def spread_copy(way, d, s):
         return remote(
@@ -166,12 +185,11 @@
 
     def chain(way, group_decays):
         order = range(members) if way == 0 else range(members - 1, -1, -1)
-        first, last = (0, groups - 1) if way == 0 else (groups - 1, 0)
-        whole = functools.reduce(lambda a, b: a * b, group_decays)
-
-        @pl.when(z == first)
-        def _():
-            carry[way] = jnp.zeros(carry.shape[1:], bf16)
+        for other in range(groups):
+
+            @pl.when(other >= z if way == 0 else other <= z)
+            def _():
+                carry[way, other] = jnp.zeros(carry.shape[2:], bf16)
 
         for s in range(pieces):
             for d in range(1, members):
@@ -180,23 +198,35 @@
             for m in order:
                 part = lrecv[way, m, s].astype(f32)
                 total = part if total is None else group_decays[m] * total + part
-
-            @pl.when(z != first)
-            def _():
-                chain_copy(way, s).wait_recv()
-
-            csend[way, s] = (whole * carry[way, s].astype(f32) + total).astype(bf16)
-
-            @pl.when(z != last)
-            def _():
-                chain_copy(way, s).start()
-
-            now = carry[way, s].astype(f32)
+            csend[way, s] = total.astype(bf16)
+            for d in range(1, groups):
+
+                @pl.when(sends_to(way, d))
+                def _():
+                    chain_copy(way, d, s).start()
+
+        if way == 0:
+            for d in range(1, groups):
+                span_arrival(d).wait_recv()
+        spans = []
+        for other in range(groups):
+            ahead = other < z if way == 0 else other > z
+            spans.append(jnp.exp(jnp.where(ahead, span_ref[other, 0:1, 0:1], 0.0)))
+        for s in range(pieces):
+            for d in range(1, groups):
+
+                @pl.when(sends_to(1 - way, d))
+                def _():
+                    chain_arrival(way, d, s).wait_recv()
+
+            now = jnp.zeros(carry.shape[3:], f32)
+            for other in range(groups) if way == 0 else range(groups - 1, -1, -1):
+                now = spans[other] * now + carry[way, other, s].astype(f32)
             for at, m in enumerate(order):
                 psend[way, m, s] = now.astype(bf16)
                 if at < members - 1:
                     now = group_decays[m] * now + lrecv[way, m, s].astype(f32)
-            for d in range(1, members):
+            for d in [members // 2, *(d for d in range(1, members) if d != members // 2)]:
                 spread_copy(way, d, s).start()
             state[way, r, s] = psend[way, r, s]
 
@@ -225,6 +255,12 @@
     for d in range(1, members):
         total_arrival(d).wait_recv()
     group_decays = [jnp.exp(total_ref[m, 0:1, 0:1]) for m in range(members)]
+    span = total_ref[0]
+    for m in range(1, members):
+        span = span + total_ref[m]
+    span_ref[z] = span
+    for d in range(1, groups):
+        span_copy(d).start()
     chain(0, group_decays)
 
     loads[4].wait()
@@ -289,12 +325,14 @@
         up_copy(d).wait_send()
     for d in range(1, groups):
         statz_copy(d).wait_send()
-    for way, last in ((0, groups - 1), (1, 0)):
-
-        @pl.when(z != last)
-        def _():
-            for s in range(pieces):
-                chain_copy(way, s).wait_send()
+        span_copy(d).wait_send()
+    for way in range(2):
+        for d in range(1, groups):
+
+            @pl.when(sends_to(way, d))
+            def _():
+                for s in range(pieces):
+                    chain_copy(way, d, s).wait_send()
 
 
 def write_out(*refs):
@@ -341,10 +379,11 @@
             pltpu.VMEM((1, dv), f32),
             pltpu.VMEM((head_total, rows // head_total, dv), bf16),
             pltpu.VMEM((members, 8, 128), f32),
+            pltpu.VMEM((groups, 8, 128), f32),
             pltpu.VMEM((2, members, dk // members, rows), bf16),
             pltpu.VMEM((2, members, *piece), bf16),
             pltpu.VMEM((2, members, *piece), bf16),
-            pltpu.VMEM((2, *piece), bf16),
+            pltpu.VMEM((2, groups, *piece), bf16),
             pltpu.VMEM((2, *piece), bf16),
             pltpu.VMEM((2, members, *piece), bf16),
             pltpu.VMEM((2, members, *piece), bf16),
@@ -355,9 +394,10 @@
             dma((2, members)),
             dma((2, max(head_total, 2))),
             dma((2, 2, members, pieces)),
-            dma((2, 2, pieces)),
+            dma((2, 2, groups, pieces)),
             dma((2, 2, members, pieces)),
             dma((2, members)),
+            dma((2, max(groups, 2))),
             dma((2, max(groups, 2))),
         ],
         compiler_params=pltpu.CompilerParams(

time: 42.6 us -> 39.7 us (0.932)
  Pallas kernels: 41.8 us -> 38.9 us
    pallas_call x1, Pallas kernels: 39.9 us -> 37 us  [shards(): pl.pallas_call(functools.partial(kernel, seq_total, head_total, members,...]
where the time goes in v3:
time: 39.7 us; the launch traced here: 39.6 us
  Pallas kernels  38.9 us (98%)
  between operations  0.64 us (2%)
    pallas_call x1, Pallas kernels, shards(): pl.pallas_call(functools.partial(kernel, seq_total, head_total, members,...  37 us
    pallas_call x1, Pallas kernels, shards(): pl.pallas_call(write_out, out_shape=shapes, in_specs=[in_vmem] * 5, out_s...  1.93 us

profile of v3, /device:TPU:0, one launch (start us, length us, event | category | flops | bytes accessed | tf_op | source)
XLA Modules:
  0.0 39.6 jit_solution(6315509816150338132)
XLA Ops:
  0.6 37.0 %shard_map.101 = (bf16[256,256]{1,0:T(8,128)(2,1)}, bf16[256,256]{1,0:T(8,128)(2,1)}, bf16[256,512]{1,0:T(8,128)(2,1)}, f32[1,512]{1,0:T(1,128)}, f32[1,512]{1,0:T(1,128)}) custom-call(bf16[256,256]{1,0:T(8,128)(2,1)} %q_hbm.1, bf16[256,256]{1,0:T(8,128)(2,1)} %k_hbm.1, bf16[256,512]{1,0:T(8,128)(2,1)} %v_hbm.1, f32[1,256]{1,0:T(1,128)} %decay_hbm.1, ...), custom_call_target="tpu_custom_call" | custom-call | tf_op jit(solution)/shard_map/pallas_call | solution.py:369
  37.7 1.9 %shard_map.102 = (bf16[256,256]{1,0:T(8,128)(2,1)}, bf16[256,256]{1,0:T(8,128)(2,1)}, bf16[256,512]{1,0:T(8,128)(2,1)}, f32[1,512]{1,0:T(1,128)}, f32[1,512]{1,0:T(1,128)}) custom-call(bf16[256,256]{1,0:T(8,128)(2,1)} %get-tuple-element.10.refs_0_, bf16[256,256]{1,0:T(8,128)(2,1)} %get-tuple-element.11.refs_1_, bf16[256,512]{1,0:T(8,128)(2,1)} %get-tuple-element.12.refs_2_, ...), custom_call_target="tpu_custom_call" | custom-call | tf_op jit(solution)/shard_map/pallas_call | solution.py:407

commit v4 on v3

--- a/solution.py
+++ b/solution.py
@@ -249,7 +249,6 @@
     decay_mat = decay_mat * scaling
     weights = (dot_nt(queries, keys) * decay_mat).astype(bf16)
     query_decayed = (queries.astype(f32) * head_decay).astype(bf16)
-    inner = dot_nn(weights, values)
     turned[1] = (scaling * query_decayed.astype(f32)).astype(bf16).T.reshape(turned.shape[1:])
 
     for d in range(1, members):
@@ -263,6 +262,7 @@
         span_copy(d).start()
     chain(0, group_decays)
 
+    inner = dot_nn(weights, values)
     loads[4].wait()
     loads[5].wait()
     for d in range(1, head_total):
@@ -285,11 +285,11 @@
     for d in range(1, members):
         stat_copy(d).start()
     grad_weights = (dot_nt(grad_output, values) * decay_mat).astype(bf16)
+    chain(1, group_decays)
+
     qg_ref[...] = (
         dot_nn(grad_weights, keys) + (scaling * head_decay) * dot_nt(grad_output, state_in)
     ).astype(bf16)
-    chain(1, group_decays)
-
     key_inner = dot_tn(grad_weights, queries)
     value_inner = dot_tn(weights, grad_output)
     for d in range(1, members):

time: 39.7 us -> 39.9 us (level)
  no operation moved by 1% of the time
where the time goes in v4:
time: 39.9 us; the launch traced here: 39.7 us
  Pallas kernels  39.1 us (98%)
  between operations  0.64 us (2%)
    pallas_call x1, Pallas kernels, shards(): pl.pallas_call(functools.partial(kernel, seq_total, head_total, members,...  37.1 us
    pallas_call x1, Pallas kernels, shards(): pl.pallas_call(write_out, out_shape=shapes, in_specs=[in_vmem] * 5, out_s...  1.93 us

profile of v4, /device:TPU:0, one launch (start us, length us, event | category | flops | bytes accessed | tf_op | source)
XLA Modules:
  0.0 39.7 jit_solution(5716024467165745617)
XLA Ops:
  0.6 37.1 %shard_map.101 = (bf16[256,256]{1,0:T(8,128)(2,1)}, bf16[256,256]{1,0:T(8,128)(2,1)}, bf16[256,512]{1,0:T(8,128)(2,1)}, f32[1,512]{1,0:T(1,128)}, f32[1,512]{1,0:T(1,128)}) custom-call(bf16[256,256]{1,0:T(8,128)(2,1)} %q_hbm.1, bf16[256,256]{1,0:T(8,128)(2,1)} %k_hbm.1, bf16[256,512]{1,0:T(8,128)(2,1)} %v_hbm.1, f32[1,256]{1,0:T(1,128)} %decay_hbm.1, ...), custom_call_target="tpu_custom_call" | custom-call | tf_op jit(solution)/shard_map/pallas_call | solution.py:369
  37.8 1.9 %shard_map.102 = (bf16[256,256]{1,0:T(8,128)(2,1)}, bf16[256,256]{1,0:T(8,128)(2,1)}, bf16[256,512]{1,0:T(8,128)(2,1)}, f32[1,512]{1,0:T(1,128)}, f32[1,512]{1,0:T(1,128)}) custom-call(bf16[256,256]{1,0:T(8,128)(2,1)} %get-tuple-element.10.refs_0_, bf16[256,256]{1,0:T(8,128)(2,1)} %get-tuple-element.11.refs_1_, bf16[256,512]{1,0:T(8,128)(2,1)} %get-tuple-element.12.refs_2_, ...), custom_call_target="tpu_custom_call" | custom-call | tf_op jit(solution)/shard_map/pallas_call | solution.py:407
